TPU v7x, 512 devices: a whole 4x4x16 slice. The times are simulated.
512 devices in a mesh: pair: 16 (over z), virt: 32 (over y, x, core).
Axes of the slice: x: 4, y: 4, z: 16, core: 2. Of those that a mesh axis runs over, the one named last changes fastest.
Arguments:
- amplitudes: bfloat16 [14336, 65536], P('pair', 'virt'), may hold values from -6 to 6
- mask_amp: int32 [112, 512], P('pair', 'virt'), may hold values from 0 to 1, as said below
- integrals: bfloat16 [65536, 1024], P('virt', 'pair'), may hold values from -0.09375 to 0.09375
- mask_int: int32 [512, 8], P('virt'), may hold values 0 or 1
Outputs:
- ladder: bfloat16 [14336, 1024], P('pair', 'virt')
Inputs may be any that keep to these rules, and one draw needn't show every extreme that they name: `mask_amp`: 1 marks an amplitude tile that is kept, 0 one that is screened out. `mask_int`: 1 marks an integral tile that is kept, 0 one that is screened out.
All inputs are finite; a program needn't handle non-finite values. No bound on the sum of `mask_int` on one device may be relied on, other than what follows from the above.
Results may differ from a plain program's by a relative error of at most 0.001.
Values may be sent and summed in bfloat16 or wider, within the bound.
No kernel may reach another device: no remote copies, remote signals or barrier semaphores. Data moves between devices by JAX's collectives and lax.ppermute only.
A program may use at most 64 MiB of HBM per device.

v0:
```python
import jax
import jax.numpy as jnp
from jax import lax
from jax.sharding import PartitionSpec as P

TILE_SIZE = 128
SLAB_TILES = 8


def shards(amplitudes, mask_amp, integrals, mask_int):
    edge_len = TILE_SIZE
    row_count, depth = amplitudes.shape
    row_tiles, depth_tiles = mask_amp.shape
    amp_mask = mask_amp.astype(jnp.bfloat16)
    amp_kept = (
        amplitudes.reshape(row_tiles, edge_len, depth_tiles, edge_len) * amp_mask[:, None, :, None]
    ).reshape(row_count, depth)
    col_mask = mask_int.astype(jnp.bfloat16)
    slab_index = jnp.arange(SLAB_TILES, dtype=jnp.int32)
    columns_in = lax.all_gather(integrals, "pair", axis=1, tiled=True)
    piece_cols = columns_in.shape[1]
    owners = jnp.arange(piece_cols, dtype=jnp.int32) // edge_len
    onehot = (owners[None, :] == slab_index[:, None]).astype(jnp.bfloat16)
    spread = jnp.dot(col_mask, onehot, preferred_element_type=jnp.float32).astype(jnp.bfloat16)
    partial_value = jnp.dot(
        amp_kept,
        (columns_in.reshape(depth_tiles, edge_len, piece_cols) * spread[:, None, :]).reshape(
            depth, piece_cols
        ),
        preferred_element_type=jnp.float32,
    )
    return lax.psum_scatter(partial_value, "virt", scatter_dimension=1, tiled=True).astype(
        jnp.bfloat16
    )


def solution(mesh):
    return jax.shard_map(
        shards,
        mesh=mesh,
        in_specs=(P("pair", "virt"), P("pair", "virt"), P("virt", "pair"), P("virt", None)),
        out_specs=P("pair", "virt"),
        check_vma=False,
    )
```

profile of v0, /device:TPU:2, one launch (start us, length us, event | category | flops | bytes accessed | tf_op | source)
XLA Modules:
  0.0 213.0 jit_solution(9740577513950336725)
XLA Ops:
  6.5 0.0 all-gather.2.cloned.1.call-start
  6.5 0.7 all-gather.2.cloned.1.call-update
  7.3 0.0 reduce-scatter.2.cloned.1.call-start
  7.3 0.7 convert_element_type.16
  8.0 0.9 fusion.3
  8.9 0.2 copy.5
  9.0 83.6 %all-gather.2.cloned.1.call-done = bf16[2048,1024]{0,1:T(8,128)(2,1)} async-done(((bf16[2048,64]{0,1:T(8,128)(2,1)}), bf16[2048,1024]{0,1:T(8,128)(2,1)}) %all-gather.2.cloned.1.call-update) | async-done | bytes 4194320 | tf_op jit(solution)/shard_map/all_gather | solution.py:20
  92.7 0.0 copy-start
  92.7 0.0 copy-start.1
  92.7 0.5 mul.22
  93.2 4.5 %mul.25 = bf16[16,128,1024]{1,0,2:T(8,128)(2,1)S(1)} broadcast(bf16[16,1024]{0,1:T(8,128)(2,1)S(1)} %copy.5), dimensions={0,2} | broadcast | bytes 4227072 | tf_op jit(solution)/shard_map/mul | solution.py:27
  97.7 0.0 copy-done
  97.7 0.0 copy-done.1
  97.7 6.4 %fusion = f32[896,1024]{0,1:T(8,128)} fusion(bf16[2048,1024]{0,1:T(8,128)(2,1)S(1)} %copy-done, bf16[128,8,16,128]{3,2,1,0:T(8,128)(2,1)S(1)} %bitcast.13, bf16[896,2048]{1,0:T(8,128)(2,1)S(1)} %copy-done.1, bf16[112,8,16,128]{3,2,1,0:T(8,128)(2,1)S(1)} %bitcast.14), kind=kOutput, calls=%fused_computation.1 | convolution fusion | flops 3762028544 | bytes 19398656 | tf_op jit(solution)/shard_map/dot_general | solution.py:25
  104.1 0.0 reduce-scatter.2.cloned.1.call-update
  104.1 100.5 %reduce-scatter.2.cloned.1.call-done = f32[896,32]{0,1:T(8,128)} async-done(((f32[896,1024]{0,1:T(8,128)}), f32[896,32]{0,1:T(8,128)}) %reduce-scatter.2.cloned.1.call-update) | async-done | bytes 114704 | tf_op jit(solution)/shard_map/reduce_scatter | solution.py:32
  204.7 1.5 convert_element_type.20
  (1 shorter events, 0.0 us)
Async XLA Ops:
  6.5 86.2 %all-gather.2.cloned.1.call-start = ((), (), s32[]{:S(2)}) async-start(), calls=%async_computation.1 | async-start | bytes 4456448 | tf_op jit(solution)/shard_map/all_gather | solution.py:20
  7.3 197.4 %reduce-scatter.2.cloned.1.call-start = ((), (), s32[]{:S(2)}) async-start(), calls=%async_computation.2 | async-start | bytes 3784704 | tf_op jit(solution)/shard_map/reduce_scatter | solution.py:32
  92.7 5.0 %copy-start = (bf16[2048,1024]{0,1:T(8,128)(2,1)S(1)}, bf16[2048,1024]{0,1:T(8,128)(2,1)}, u32[]{:S(2)}) copy-start(bf16[2048,1024]{0,1:T(8,128)(2,1)} %all-gather.2.cloned.1.call-done) | copy-start | bytes 12582916
  92.7 5.0 %copy-start.1 = (bf16[896,2048]{1,0:T(8,128)(2,1)S(1)}, bf16[896,2048]{1,0:T(8,128)(2,1)}, u32[]{:S(2)}) copy-start(bf16[896,2048]{1,0:T(8,128)(2,1)} %param.4) | copy-start | bytes 11010052
Sparse Core Ops, SparseCore 0:
  9.4 83.2 all-gather.1
  104.2 100.3 reduce-scatter.1
where the time goes:
time: 213 us
  waiting for transfers between devices  185 us (87%)
  between operations  13.4 us (6%)
  matrix products  7.23 us (3%)
  local copies, waits for them, and re-layouts  5.18 us (2%)
  other arithmetic  2.22 us (1%)
    reduce_scatter x1, waiting for transfers between devices, shards(): lax.psum_scatter(partial_value, 'virt', scatter_dimension=1, tiled=True)  101 us
    all_gather x1, waiting for transfers between devices, shards(): columns_in = lax.all_gather(integrals, 'pair', axis=1, tiled=True)  83.6 us
    dot_general x1, matrix products, shards(): jnp.dot(amp_kept, (columns_in.reshape(depth_tiles, edge_len, piece_cols)...  6.36 us
    mul x1, local copies, waits for them, and re-layouts, shards(): columns_in.reshape(depth_tiles, edge_len, piece_cols) * spread[:, None, :]  4.46 us
  transfers between devices with their start and end apart: 2, of which 2 were waited for; matrix products, arithmetic and copies ran while one was open for 1% of the time, Pallas kernels for 0%

commit v1 on v0

v1 whole, which is shorter than its diff:
```python
import jax
import jax.numpy as jnp
from jax import lax
from jax.sharding import Mesh, PartitionSpec as P

TILE_SIZE = 128
PLANE = ("y", "x")
LEVELS = 7
LIFT = 2.0**16
FIRST_SCALE = 2.0**18
FIRST_LIMIT = 2.0**-19


def column_levels(largest):
    level = jnp.zeros_like(largest)
    for step in range(LEVELS - 1):
        level = jnp.where(largest < FIRST_LIMIT * LIFT**-step, step + 1.0, level)
    return level


def of_level(level, sign):
    value = jnp.full_like(level, FIRST_SCALE**sign)
    for step in range(1, LEVELS):
        value = jnp.where(level == step, (FIRST_SCALE * LIFT**step) ** sign, value)
    return value


def shards(amplitudes, mask_amp, integrals, mask_int):
    row_tiles, depth_tiles = mask_amp.shape
    depth, width = integrals.shape
    half = width // 2
    pair, core = lax.axis_index("pair"), lax.axis_index("core")
    other = [(0, 1), (1, 0)]

    kept = lax.dynamic_slice_in_dim(mask_int, pair * width // TILE_SIZE, 1, 1)[:, 0]
    columns = integrals.T.astype(jnp.float32).reshape(width, depth_tiles, TILE_SIZE)
    columns = (columns * kept.astype(jnp.float32)[None, :, None]).reshape(width, depth)
    level = column_levels(jnp.max(jnp.abs(columns), axis=1, keepdims=True))
    coded = (columns * of_level(level, 1)).astype(jnp.float16)
    coded = jnp.concatenate(
        [coded, jnp.broadcast_to(level, (width, TILE_SIZE)).astype(jnp.float16)], axis=1
    )
    mine = lax.dynamic_slice_in_dim(coded, core * half, half, 0)
    theirs = lax.ppermute(lax.dynamic_slice_in_dim(coded, (1 - core) * half, half, 0), "core", other)

    amp_mask = mask_amp.astype(jnp.bfloat16)
    amp_kept = (
        amplitudes.reshape(row_tiles, TILE_SIZE, depth_tiles, TILE_SIZE) * amp_mask[:, None, :, None]
    ).reshape(amplitudes.shape)
    amp_theirs = lax.ppermute(amp_kept, "core", other)

    sent = jnp.concatenate(
        [mine[:, :depth], theirs[:, :depth], mine[:, depth : depth + 64], theirs[:, depth : depth + 64]],
        axis=1,
    )
    slab = lax.all_gather(sent, "pair", axis=0, tiled=True)

    def product(start, level_at, amps):
        block = slab[:, start : start + depth].astype(jnp.bfloat16)
        scale = of_level(slab[:, level_at : level_at + 1].astype(jnp.float32), -1)
        return scale * lax.dot_general(
            block, amps, (((1,), (1,)), ((), ())), preferred_element_type=jnp.float32
        )

    partial_value = product(0, 2 * depth, amp_kept) + product(depth, 2 * depth + 64, amp_theirs)
    pieces = lax.all_to_all(partial_value, PLANE, 0, 0, tiled=True)
    total = jnp.sum(pieces.reshape(-1, half, pieces.shape[1]), axis=0)
    return total.astype(jnp.bfloat16).T


def solution(mesh):
    grid = Mesh(mesh.devices.reshape(-1, 4, 4, 2), ("pair", "y", "x", "core"))
    virt = ("y", "x", "core")
    return jax.shard_map(
        shards,
        mesh=grid,
        in_specs=(P("pair", virt), P("pair", virt), P(virt, "pair"), P(virt, None)),
        out_specs=P("pair", virt),
        check_vma=False,
    )
```

time: 213 us -> 118 us (0.55)
  the two profiles are of different devices: /device:TPU:2 before, /device:TPU:32 now
where the time goes in v1:
time: 118 us; the launch traced here: 117 us
  blocking collectives  94.1 us (80%)
  matrix products  8.88 us (8%)
  other arithmetic  5.55 us (5%)
  starting transfers between devices  4.32 us (4%)
  waiting for transfers between devices  2.87 us (2%)
  local copies, waits for them, and re-layouts  1.56 us (1%)
    all_gather x1, blocking collectives, shards(): slab = lax.all_gather(sent, 'pair', axis=0, tiled=True)  66.2 us
    all_to_all x1, blocking collectives, shards(): pieces = lax.all_to_all(partial_value, PLANE, 0, 0, tiled=True)  27.8 us
    dot_general x2, matrix products, product(): lax.dot_general(block, amps, (((1,), (1,)), ((), ())), preferred_element_...  8.88 us
    ppermute x1, waiting for transfers between devices, shards(): lax.ppermute(lax.dynamic_slice_in_dim(coded, (1 - core) * half, half, 0),...  2.87 us
    mul x1, other arithmetic, shards(): amplitudes.reshape(row_tiles, TILE_SIZE, depth_tiles, TILE_SIZE)  2.6 us
    ppermute x1, starting transfers between devices, shards(): lax.ppermute(lax.dynamic_slice_in_dim(coded, (1 - core) * half, half, 0),...  2.41 us
  transfers between devices with their start and end apart: 2, of which 1 were waited for; matrix products, arithmetic and copies ran while one was open for 5% of the time, Pallas kernels for 0%

profile of v1, /device:TPU:32, one launch (start us, length us, event | category | flops | bytes accessed | tf_op | source)
XLA Modules:
  0.0 117.4 jit_solution(1694411313858969528)
XLA Ops:
  0.0 0.0 copy-start
  0.0 0.8 convert_element_type.54
  0.8 0.5 mul.74
  1.4 0.7 copy-done
  2.1 0.0 copy-start.1
  2.1 2.6 %bitcast_multiply_fusion = bf16[896,2048]{1,0:T(8,128)(2,1)} fusion(bf16[896,2048]{1,0:T(8,128)(2,1)S(1)} %copy-done, bf16[112,8,16,128]{3,2,1,0:T(8,128)(2,1)S(1)} %bitcast.16), kind=kLoop, calls=%fused_computation | loop fusion | flops 1835008 | bytes 11010048 | tf_op jit(solution)/shard_map/mul | solution.py:48
  4.7 1.9 %collective-permute-start.1 = (bf16[896,2048]{1,0:T(8,128)(2,1)}, bf16[896,2048]{1,0:T(8,128)(2,1)}, u32[]{:S(2)}, u32[]{:S(2)}) collective-permute-start(bf16[896,2048]{1,0:T(8,128)(2,1)} %bitcast_multiply_fusion), channel_id=1, source_target_pairs={{0,1},{1,0},{2,3},{3,2},{4,5},{5,4},{6,7},{7,6},{8,9},{9,8},{10,11... | collective-permute-start | bytes 11010056 | tf_op jit(solution)/shard_map/ppermute | solution.py:50
  6.6 0.7 fusion.6
  7.3 0.1 broadcast_bitcast_fusion
  7.4 0.0 copy-done.1
  7.4 0.2 abs_reduce_fusion
  7.5 0.1 fusion.2
  7.7 0.1 broadcast_in_dim.90
  7.7 0.1 fusion.3
  7.8 2.4 %collective-permute-start = (f16[32,2176]{1,0:T(8,128)(2,1)S(1)}, f16[32,2176]{1,0:T(8,128)(2,1)S(1)}, u32[]{:S(2)}, u32[]{:S(2)}) collective-permute-start(f16[32,2176]{1,0:T(8,128)(2,1)S(1)} %get-tuple-element.9), channel_id=1, source_target_pairs={{0,1},{1,0},{2,3},{3,2},{4,5},{5,4},{6,7},{7,6},{8,9},{9,8},{10,11... | collective-permute-start | bytes 417800 | tf_op jit(solution)/shard_map/ppermute | solution.py:44
  10.3 2.9 %collective-permute-done = f16[32,2176]{1,0:T(8,128)(2,1)S(1)} collective-permute-done((f16[32,2176]{1,0:T(8,128)(2,1)S(1)}, f16[32,2176]{1,0:T(8,128)(2,1)S(1)}, u32[]{:S(2)}, u32[]{:S(2)}) %collective-permute-start) | collective-permute-done | bytes 139296 | tf_op jit(solution)/shard_map/ppermute | solution.py:44
  13.2 0.1 concatenate.7
  13.3 66.2 %all-gather.1 = f16[512,4224]{1,0:T(8,128)(2,1)S(1)} all-gather(f16[32,4224]{1,0:T(8,128)(2,1)S(1)} %concatenate.7), channel_id=1, replica_groups=mesh['pair'=16,'y'=4,'x'=4,'core'=2] {'pair'}, dimensions={0}, use_global_device_ids=true | all-gather | bytes 4595712 | tf_op jit(solution)/shard_map/all_gather | solution.py:56
  79.5 0.3 select_reduce_fusion.1
  79.9 4.4 %fusion.1 = f32[512,896]{1,0:T(8,128)S(1)} fusion(bf16[896,2048]{1,0:T(8,128)(2,1)} %bitcast_multiply_fusion, f16[512,4224]{1,0:T(8,128)(2,1)S(1)} %all-gather.1), kind=kOutput, calls=%fused_computation.4 | convolution fusion | flops 1880096768 | bytes 7602176 | tf_op jit(solution)/shard_map/dot_general | solution.py:61
  84.3 0.0 collective-permute-done.1
  84.3 4.5 %multiply_add_fusion = f32[512,896]{1,0:T(8,128)S(1)} fusion(f32[512,896]{1,0:T(8,128)S(1)} %fusion.1, bf16[896,2048]{1,0:T(8,128)(2,1)} %collective-permute-done.1, f16[512,4224]{1,0:T(8,128)(2,1)S(1)} %all-gather.1, f32[512]{0:T(512)S(1)} %get-tuple-element.6, f32[512]{0:T(512)S(1)} %get-tuple-element.5), kind=kOutput, calls=%fused_computation.5 | convolution fusion | flops 1881473024 | bytes 9441280 | tf_op jit(solution)/shard_map/dot_general | solution.py:61
  88.8 27.8 %all_to_all.9 = f32[16,32,896]{2,1,0:T(8,128)S(1)} all-to-all(f32[16,32,896]{2,1,0:T(8,128)S(1)} %bitcast.17), channel_id=1, replica_groups=mesh['pair'=16,'y'=4,'x'=4,'core'=2] {'y','x'}, dimensions={0} | all-to-all | bytes 3670016 | tf_op jit(solution)/shard_map/all_to_all | solution.py:66
  116.6 0.7 reduce_sum.9
  (6 shorter events, 0.1 us)
Async XLA Ops:
  0.0 2.1 %copy-start = (bf16[896,2048]{1,0:T(8,128)(2,1)S(1)}, bf16[896,2048]{1,0:T(8,128)(2,1)}, u32[]{:S(2)}) copy-start(bf16[896,2048]{1,0:T(8,128)(2,1)} %param.4) | copy-start | bytes 11010052
  2.1 5.3 %copy-start.1 = (bf16[2048,64]{0,1:T(8,128)(2,1)S(1)}, bf16[2048,64]{0,1:T(8,128)(2,1)}, u32[]{:S(2)}) copy-start(bf16[2048,64]{0,1:T(8,128)(2,1)} %param.6) | copy-start | bytes 786436
  4.7 79.7 %collective-permute-start.1 = (bf16[896,2048]{1,0:T(8,128)(2,1)}, bf16[896,2048]{1,0:T(8,128)(2,1)}, u32[]{:S(2)}, u32[]{:S(2)}) collective-permute-start(bf16[896,2048]{1,0:T(8,128)(2,1)} %bitcast_multiply_fusion), channel_id=1, source_target_pairs={{0,1},{1,0},{2,3},{3,2},{4,5},{5,4},{6,7},{7,6},{8,9},{9,8},{10,11... | collective-permute-start | bytes 11010056 | tf_op jit(solution)/shard_map/ppermute | solution.py:50
  7.8 5.3 %collective-permute-start = (f16[32,2176]{1,0:T(8,128)(2,1)S(1)}, f16[32,2176]{1,0:T(8,128)(2,1)S(1)}, u32[]{:S(2)}, u32[]{:S(2)}) collective-permute-start(f16[32,2176]{1,0:T(8,128)(2,1)S(1)} %get-tuple-element.9), channel_id=1, source_target_pairs={{0,1},{1,0},{2,3},{3,2},{4,5},{5,4},{6,7},{7,6},{8,9},{9,8},{10,11... | collective-permute-start | bytes 417800 | tf_op jit(solution)/shard_map/ppermute | solution.py:44

commit v2 on v1

v2 whole, which is shorter than its diff:
```python
import jax
import jax.numpy as jnp
from jax import lax
from jax.experimental import pallas as pl
from jax.experimental.pallas import tpu as pltpu
from jax.sharding import Mesh, PartitionSpec as P

TILE_SIZE = 128
PLANE = ("y", "x")
OTHER_CORE = [(0, 1), (1, 0)]
LEVELS = 7
LIFT = 2.0**16
FIRST_SCALE = 2.0**18
FIRST_LIMIT = 2.0**-19


def column_levels(largest):
    level = jnp.zeros_like(largest)
    for step in range(LEVELS - 1):
        level = jnp.where(largest < FIRST_LIMIT * LIFT**-step, step + 1.0, level)
    return level


def of_level(level, sign):
    value = jnp.full_like(level, FIRST_SCALE**sign)
    for step in range(1, LEVELS):
        value = jnp.where(level == step, (FIRST_SCALE * LIFT**step) ** sign, value)
    return value


def lowered(steps):
    value = jnp.ones_like(steps)
    for step in range(1, LEVELS):
        value = jnp.where(steps == step, LIFT**-step, value)
    return value


def prepared(columns_ref, keep_amp_ref, keep_ref, stay_ref, away_ref, kept_ref, tail_ref):
    width, depth = columns_ref.shape
    half = width // 2
    slab = lax.axis_index("pair") // (TILE_SIZE // width)
    first = lax.axis_index("core") == 0
    largest = jnp.zeros((width, TILE_SIZE), jnp.float32)
    for tile in range(depth // TILE_SIZE):
        at = slice(tile * TILE_SIZE, (tile + 1) * TILE_SIZE)
        block = columns_ref[:, at].astype(jnp.float32) * keep_ref[slab, tile].astype(jnp.float32)
        kept_ref[:, at] = block
        largest = jnp.maximum(largest, jnp.abs(block))
    level = column_levels(jnp.max(largest, axis=1, keepdims=True))
    scaled = kept_ref[...] * of_level(level, 1)
    lower, upper = scaled[:half], scaled[half:]
    stay_ref[:, :depth] = jnp.where(first, lower, upper).astype(jnp.bfloat16)
    away_ref[:, :depth] = jnp.where(first, upper, lower).astype(jnp.bfloat16)
    level = jnp.broadcast_to(level, (width, TILE_SIZE))
    lower, upper = level[:half], level[half:]
    stay_ref[:, depth:] = jnp.where(first, lower, upper).astype(jnp.bfloat16)
    away_ref[:, depth : depth + TILE_SIZE] = jnp.where(first, upper, lower).astype(jnp.bfloat16)
    tail_ref[...] = jnp.zeros_like(tail_ref)
    tail_ref[: keep_amp_ref.shape[0], : keep_amp_ref.shape[1]] = keep_amp_ref[...].astype(jnp.float32)
    away_ref[:, depth + TILE_SIZE :] = tail_ref[...].astype(jnp.bfloat16)


def masked_product(columns_ref, mine_ref, theirs_ref, keep_mine_ref, keep_theirs_ref, out_ref, kept_ref, sems):
    depth = mine_ref.shape[1]
    loads = [
        pltpu.make_async_copy(amps, kept_ref.at[part], sems.at[part]) for part, amps in enumerate((mine_ref, theirs_ref))
    ]
    for load in loads:
        load.start()
    scale = of_level(columns_ref[:, 2 * depth : 2 * depth + 1].astype(jnp.float32), -1)
    for part, keep in enumerate((keep_mine_ref, keep_theirs_ref)):
        loads[part].wait()
        for row_tile in range(keep.shape[0]):
            for tile in range(keep.shape[1]):
                rows = slice(row_tile * TILE_SIZE, (row_tile + 1) * TILE_SIZE)
                at = slice(tile * TILE_SIZE, (tile + 1) * TILE_SIZE)
                kept_ref[part, rows, at] *= keep[row_tile, tile].astype(jnp.bfloat16)
    out_ref[...] = scale * sum(
        lax.dot_general(
            columns_ref[:, part * depth : (part + 1) * depth],
            kept_ref[part],
            (((1,), (1,)), ((), ())),
            preferred_element_type=jnp.float32,
        )
        for part in range(2)
    )


def shards(amplitudes, mask_amp, integrals, mask_int):
    row_tiles, depth_tiles = mask_amp.shape
    rows = amplitudes.shape[0]
    depth, width = integrals.shape
    half = width // 2

    vmem, smem = pl.BlockSpec(memory_space=pltpu.VMEM), pl.BlockSpec(memory_space=pltpu.SMEM)
    hbm = pl.BlockSpec(memory_space=pltpu.HBM)
    stay, away = pl.pallas_call(
        prepared,
        out_shape=(
            pltpu.VMEM((half, depth + TILE_SIZE), jnp.bfloat16),
            pltpu.VMEM((half, depth + 2 * TILE_SIZE), jnp.bfloat16),
        ),
        in_specs=[vmem, vmem, smem],
        out_specs=(vmem, vmem),
        scratch_shapes=[
            pltpu.VMEM((width, depth), jnp.float32),
            pltpu.VMEM((half, TILE_SIZE), jnp.float32),
        ],
    )(integrals.T, mask_amp, mask_int.T)
    theirs = lax.ppermute(away, "core", OTHER_CORE)
    amplitudes, stay = lax.optimization_barrier((amplitudes, stay))
    amp_theirs = lax.ppermute(amplitudes, "core", OTHER_CORE)
    keep_at = depth + TILE_SIZE
    keep_theirs = theirs[:row_tiles, keep_at : keep_at + depth_tiles].astype(jnp.int32)

    levels = [part[:, depth : depth + 1].astype(jnp.float32) for part in (stay, theirs)]
    level = jnp.minimum(*levels)
    sent = jnp.concatenate(
        [part[:, :depth].astype(jnp.float32) * lowered(own - level) for part, own in zip((stay, theirs), levels)]
        + [jnp.broadcast_to(level, (half, TILE_SIZE))],
        axis=1,
    ).astype(jnp.float16)
    columns = lax.all_gather(sent, "pair", axis=0, tiled=True).astype(jnp.bfloat16)

    partial_value = pl.pallas_call(
        masked_product,
        out_shape=jax.ShapeDtypeStruct((columns.shape[0], rows), jnp.float32),
        in_specs=[vmem, hbm, hbm, smem, smem],
        out_specs=vmem,
        scratch_shapes=[
            pltpu.VMEM((2, rows, depth), jnp.bfloat16),
            pltpu.SemaphoreType.DMA((2,)),
        ],
        compiler_params=pltpu.CompilerParams(vmem_limit_bytes=32 * 1024 * 1024),
        cost_estimate=pl.CostEstimate(
            flops=4 * columns.shape[0] * rows * depth, bytes_accessed=16 * 1024 * 1024, transcendentals=0
        ),
    )(columns, amplitudes, amp_theirs, mask_amp, keep_theirs)
    pieces = lax.all_to_all(partial_value, PLANE, 0, 0, tiled=True)
    total = jnp.sum(pieces.reshape(-1, half, pieces.shape[1]), axis=0)
    return total.astype(jnp.bfloat16).T


def solution(mesh):
    grid = Mesh(mesh.devices.reshape(-1, 4, 4, 2), ("pair", "y", "x", "core"))
    virt = ("y", "x", "core")
    return jax.shard_map(
        shards,
        mesh=grid,
        in_specs=(P("pair", virt), P("pair", virt), P(virt, "pair"), P(virt, None)),
        out_specs=P("pair", virt),
        check_vma=False,
    )
```

time: 118 us -> 111 us (0.941)
  matrix products: 8.88 us -> 0 us
  Pallas kernels: 0 us -> 8.41 us
  other arithmetic: 5.55 us -> 1.81 us
  waiting for transfers between devices: 2.87 us -> 0.01 us
    dot_general x2 -> x0, matrix products: 8.88 us -> none  [product(): lax.dot_general(block, amps, (((1,), (1,)), ((), ())), preferred_element_...]
    pallas_call x0 -> x2, Pallas kernels: none -> 8.41 us  [the longest x1 7.22 us: shards(): pl.pallas_call(masked_product, out_shape=jax.ShapeDtypeStruct((columns.sh...]
    ppermute x2, waiting for transfers between devices: 2.87 us -> 0.01 us  [the longest x1 0.01 us: shards(): amp_theirs = lax.ppermute(amplitudes, 'core', OTHER_CORE)]
    mul x1 -> x0, other arithmetic: 2.6 us -> none  [shards(): amplitudes.reshape(row_tiles, TILE_SIZE, depth_tiles, TILE_SIZE)]
  transfers between devices with their start and end apart: 2 -> 2, of which waited for: 1 -> 0; matrix products, arithmetic and copies ran while one was open for 5% -> 1% of each run, Pallas kernels for 0% -> 0%
where the time goes in v2:
time: 111 us
  blocking collectives  94.5 us (85%)
  Pallas kernels  8.41 us (8%)
  starting transfers between devices  4.33 us (4%)
  other arithmetic  1.81 us (2%)
  local copies, waits for them, and re-layouts  1.54 us (1%)
    all_gather x1, blocking collectives, shards(): lax.all_gather(sent, 'pair', axis=0, tiled=True).astype(jnp.bfloat16)  66.6 us
    all_to_all x1, blocking collectives, shards(): pieces = lax.all_to_all(partial_value, PLANE, 0, 0, tiled=True)  27.9 us
    pallas_call x1, Pallas kernels, shards(): pl.pallas_call(masked_product, out_shape=jax.ShapeDtypeStruct((columns.sh...  7.22 us
    ppermute x1, starting transfers between devices, shards(): amp_theirs = lax.ppermute(amplitudes, 'core', OTHER_CORE)  2.41 us
  transfers between devices with their start and end apart: 2, of which 0 were waited for; matrix products, arithmetic and copies ran while one was open for 1% of the time, Pallas kernels for 0%

profile of v2, /device:TPU:32, one launch (start us, length us, event | category | flops | bytes accessed | tf_op | source)
XLA Modules:
  0.0 110.7 jit_solution(13434787116638239541)
XLA Ops:
  0.0 1.2 %shard_map.46 = (bf16[32,2176]{1,0:T(8,128)(2,1)S(1)}, bf16[32,2304]{1,0:T(8,128)(2,1)S(1)}) custom-call(bf16[64,2048]{1,0:T(8,128)(2,1)} %bitcast.7, s32[7,16]{1,0:T(8,128)} %keep_mine_ref.1, s32[8,16]{1,0:T(8,128)} %bitcast.8), custom_call_target="tpu_custom_call" | custom-call | tf_op jit(solution)/shard_map/pallas_call | solution.py:97
  1.2 1.9 %collective-permute-start = (bf16[32,2304]{1,0:T(8,128)(2,1)S(1)}, bf16[32,2304]{1,0:T(8,128)(2,1)S(1)}, u32[]{:S(2)}, u32[]{:S(2)}) collective-permute-start(bf16[32,2304]{1,0:T(8,128)(2,1)S(1)} %get-tuple-element.11), channel_id=1, source_target_pairs={{0,1},{1,0},{2,3},{3,2},{4,5},{5,4},{6,7},{7,6},{8,9},{9,8},{10,11... | collective-permute-start | bytes 442376 | tf_op jit(solution)/shard_map/ppermute | solution.py:110
  3.1 2.4 %collective-permute-start.1 = (bf16[896,2048]{1,0:T(8,128)(2,1)}, bf16[896,2048]{1,0:T(8,128)(2,1)S(1)}, u32[]{:S(2)}, u32[]{:S(2)}) collective-permute-start(bf16[896,2048]{1,0:T(8,128)(2,1)} %mine_ref), channel_id=1, source_target_pairs={{0,1},{1,0},{2,3},{3,2},{4,5},{5,4},{6,7},{7,6},{8,9},{9,8},{10,11... | collective-permute-start | bytes 11010056 | tf_op jit(solution)/shard_map/ppermute | solution.py:112
  5.5 0.0 collective-permute-done
  5.6 0.1 select_reduce_fusion.1
  5.7 0.1 fusion.1
  5.8 0.1 multiply_convert_fusion.1
  5.9 0.1 multiply_convert_fusion
  6.0 0.1 broadcast_in_dim.39
  6.1 0.1 pad_maximum_fusion
  6.2 66.6 %all-gather.1 = f16[512,4224]{1,0:T(8,128)(2,1)S(1)} all-gather(f16[32,4224]{1,0:T(8,128)(2,1)S(1)} %pad_maximum_fusion), channel_id=1, replica_groups=mesh['pair'=16,'y'=4,'x'=4,'core'=2] {'pair'}, dimensions={0}, use_global_device_ids=true | all-gather | bytes 4595712 | tf_op jit(solution)/shard_map/all_gather | solution.py:123
  72.8 0.0 copy-start
  72.8 0.0 copy-start.1
  72.8 0.6 convert_element_type.30.columns_ref
  73.4 0.0 collective-permute-done.1.theirs_ref
  73.4 0.1 copy-done
  73.5 1.4 %copy-done.1 = bf16[896,2048]{1,0:T(8,128)(2,1)S(1)} copy-done((bf16[896,2048]{1,0:T(8,128)(2,1)S(1)}, bf16[896,2048]{1,0:T(8,128)(2,1)}, u32[]{:S(2)}) %copy-start.1) | copy-done | bytes 3670040
  74.8 7.2 %shard_map.47 = f32[512,896]{1,0:T(8,128)S(1)} custom-call(bf16[512,4224]{1,0:T(8,128)(2,1)S(1)} %convert_element_type.30.columns_ref, bf16[896,2048]{1,0:T(8,128)(2,1)S(1)} %copy-done.1, bf16[896,2048]{1,0:T(8,128)(2,1)S(1)} %collective-permute-done.1.theirs_ref, s32[7,16]{1,0:T(8,128)S(1)} %copy-done, s32[7,16]{1,0:T(8,128)S(1)} %slice_convert_fusion.keep_theirs_ref), custom_call_target="tpu_custom_call" | custom-call | flops 3758096384 | bytes 16777216 | tf_op jit(solution)/shard_map/pallas_call | solution.py:125
  82.1 27.9 %all_to_all.9 = f32[16,32,896]{2,1,0:T(8,128)S(1)} all-to-all(f32[16,32,896]{2,1,0:T(8,128)S(1)} %bitcast.6), channel_id=1, replica_groups=mesh['pair'=16,'y'=4,'x'=4,'core'=2] {'y','x'}, dimensions={0} | all-to-all | bytes 3670016 | tf_op jit(solution)/shard_map/all_to_all | solution.py:139
  110.0 0.7 reduce_sum.9
  (1 shorter events, 0.0 us)
Async XLA Ops:
  1.2 4.3 %collective-permute-start = (bf16[32,2304]{1,0:T(8,128)(2,1)S(1)}, bf16[32,2304]{1,0:T(8,128)(2,1)S(1)}, u32[]{:S(2)}, u32[]{:S(2)}) collective-permute-start(bf16[32,2304]{1,0:T(8,128)(2,1)S(1)} %get-tuple-element.11), channel_id=1, source_target_pairs={{0,1},{1,0},{2,3},{3,2},{4,5},{5,4},{6,7},{7,6},{8,9},{9,8},{10,11... | collective-permute-start | bytes 442376 | tf_op jit(solution)/shard_map/ppermute | solution.py:110
  3.1 70.2 %collective-permute-start.1 = (bf16[896,2048]{1,0:T(8,128)(2,1)}, bf16[896,2048]{1,0:T(8,128)(2,1)S(1)}, u32[]{:S(2)}, u32[]{:S(2)}) collective-permute-start(bf16[896,2048]{1,0:T(8,128)(2,1)} %mine_ref), channel_id=1, source_target_pairs={{0,1},{1,0},{2,3},{3,2},{4,5},{5,4},{6,7},{7,6},{8,9},{9,8},{10,11... | collective-permute-start | bytes 11010056 | tf_op jit(solution)/shard_map/ppermute | solution.py:112
  72.8 0.7 copy-start
  72.8 2.1 %copy-start.1 = (bf16[896,2048]{1,0:T(8,128)(2,1)S(1)}, bf16[896,2048]{1,0:T(8,128)(2,1)}, u32[]{:S(2)}) copy-start(bf16[896,2048]{1,0:T(8,128)(2,1)} %mine_ref) | copy-start | bytes 11010052

commit v3 on v2

--- a/solution.py
+++ b/solution.py
@@ -12,6 +12,10 @@
 LIFT = 2.0**16
 FIRST_SCALE = 2.0**18
 FIRST_LIMIT = 2.0**-19
+STEPS = 32000.0
+OCTAVE = 8.0
+CODE_ROWS = 16
+SMALLEST = 1e-33
 
 
 def column_levels(largest):
@@ -60,7 +64,9 @@
     away_ref[:, depth + TILE_SIZE :] = tail_ref[...].astype(jnp.bfloat16)
 
 
-def masked_product(columns_ref, mine_ref, theirs_ref, keep_mine_ref, keep_theirs_ref, out_ref, kept_ref, sems):
+def masked_product(
+    columns_ref, mine_ref, theirs_ref, keep_mine_ref, keep_theirs_ref, out_ref, kept_ref, total_ref, code_ref, sems
+):
     depth = mine_ref.shape[1]
     loads = [
         pltpu.make_async_copy(amps, kept_ref.at[part], sems.at[part]) for part, amps in enumerate((mine_ref, theirs_ref))
@@ -75,7 +81,7 @@
                 rows = slice(row_tile * TILE_SIZE, (row_tile + 1) * TILE_SIZE)
                 at = slice(tile * TILE_SIZE, (tile + 1) * TILE_SIZE)
                 kept_ref[part, rows, at] *= keep[row_tile, tile].astype(jnp.bfloat16)
-    out_ref[...] = scale * sum(
+    total_ref[...] = scale * sum(
         lax.dot_general(
             columns_ref[:, part * depth : (part + 1) * depth],
             kept_ref[part],
@@ -84,6 +90,26 @@
         )
         for part in range(2)
     )
+    pieces, row_tiles = out_ref.shape[0], keep_mine_ref.shape[0]
+    half = columns_ref.shape[0] // pieces
+
+    def block(piece, tile):
+        return total_ref[piece * half : (piece + 1) * half, tile * TILE_SIZE : (tile + 1) * TILE_SIZE]
+
+    code_ref[...] = jnp.zeros_like(code_ref)
+    for piece in range(pieces):
+        for tile in range(row_tiles):
+            largest = jnp.max(jnp.abs(block(piece, tile)), axis=0, keepdims=True)
+            code_ref[piece * CODE_ROWS + tile : piece * CODE_ROWS + tile + 1, :] = largest
+    codes = jnp.ceil(jnp.log2(jnp.maximum(code_ref[...], SMALLEST) / STEPS) * OCTAVE)
+    code_ref[...] = jnp.exp2(codes * (-1.0 / OCTAVE))
+    codes = codes.astype(jnp.int32).astype(jnp.int16)
+    for piece in range(pieces):
+        for tile in range(row_tiles):
+            inverse = code_ref[piece * CODE_ROWS + tile : piece * CODE_ROWS + tile + 1, :]
+            fixed = jnp.round(block(piece, tile) * inverse).astype(jnp.int32).astype(jnp.int16)
+            out_ref[piece, tile * half : (tile + 1) * half, :] = fixed
+        out_ref[piece, row_tiles * half :, :] = codes[piece * CODE_ROWS : (piece + 1) * CODE_ROWS]
 
 
 def shards(amplitudes, mask_amp, integrals, mask_int):
@@ -122,13 +148,16 @@
     ).astype(jnp.float16)
     columns = lax.all_gather(sent, "pair", axis=0, tiled=True).astype(jnp.bfloat16)
 
+    pieces = columns.shape[0] // half
     partial_value = pl.pallas_call(
         masked_product,
-        out_shape=jax.ShapeDtypeStruct((columns.shape[0], rows), jnp.float32),
+        out_shape=jax.ShapeDtypeStruct((pieces, row_tiles * half + CODE_ROWS, TILE_SIZE), jnp.int16),
         in_specs=[vmem, hbm, hbm, smem, smem],
         out_specs=vmem,
         scratch_shapes=[
             pltpu.VMEM((2, rows, depth), jnp.bfloat16),
+            pltpu.VMEM((columns.shape[0], rows), jnp.float32),
+            pltpu.VMEM((pieces * CODE_ROWS, TILE_SIZE), jnp.float32),
             pltpu.SemaphoreType.DMA((2,)),
         ],
         compiler_params=pltpu.CompilerParams(vmem_limit_bytes=32 * 1024 * 1024),
@@ -136,9 +165,11 @@
             flops=4 * columns.shape[0] * rows * depth, bytes_accessed=16 * 1024 * 1024, transcendentals=0
         ),
     )(columns, amplitudes, amp_theirs, mask_amp, keep_theirs)
-    pieces = lax.all_to_all(partial_value, PLANE, 0, 0, tiled=True)
-    total = jnp.sum(pieces.reshape(-1, half, pieces.shape[1]), axis=0)
-    return total.astype(jnp.bfloat16).T
+    partial_value = lax.all_to_all(partial_value, PLANE, 0, 0, tiled=True).astype(jnp.float32)
+    steps = jnp.exp2(partial_value[:, row_tiles * half : row_tiles * half + row_tiles] * (1.0 / OCTAVE))
+    fixed = partial_value[:, : row_tiles * half].reshape(pieces, row_tiles, half, TILE_SIZE)
+    total = jnp.sum(fixed * steps[:, :, None, :], axis=0)
+    return total.astype(jnp.bfloat16).transpose(0, 2, 1).reshape(rows, half)
 
 
 def solution(mesh):

time: 111 us -> 104 us (0.937)
  the two profiles are of different devices: /device:TPU:32 before, /device:TPU:2 now
where the time goes in v3:
time: 104 us
  blocking collectives  86.7 us (83%)
  Pallas kernels  8.74 us (8%)
  starting transfers between devices  4.33 us (4%)
  local copies, waits for them, and re-layouts  2.18 us (2%)
  other arithmetic  1.5 us (1%)
    all_gather x1, blocking collectives, shards(): lax.all_gather(sent, 'pair', axis=0, tiled=True).astype(jnp.bfloat16)  68.1 us
    all_to_all x1, blocking collectives, shards(): lax.all_to_all(partial_value, PLANE, 0, 0, tiled=True).astype(jnp.float32)  18.6 us
    pallas_call x1, Pallas kernels, shards(): pl.pallas_call(masked_product, out_shape=jax.ShapeDtypeStruct((pieces, ro...  7.55 us
    ppermute x1, starting transfers between devices, shards(): amp_theirs = lax.ppermute(amplitudes, 'core', OTHER_CORE)  2.41 us
  transfers between devices with their start and end apart: 2, of which 0 were waited for; matrix products, arithmetic and copies ran while one was open for 1% of the time, Pallas kernels for 0%

profile of v3, /device:TPU:2, one launch (start us, length us, event | category | flops | bytes accessed | tf_op | source)
XLA Modules:
  0.0 103.5 jit_solution(6769322921270611186)
XLA Ops:
  0.0 1.2 %shard_map.46 = (bf16[32,2176]{1,0:T(8,128)(2,1)S(1)}, bf16[32,2304]{1,0:T(8,128)(2,1)S(1)}) custom-call(bf16[64,2048]{1,0:T(8,128)(2,1)} %bitcast.11, s32[7,16]{1,0:T(8,128)} %keep_mine_ref.1, s32[8,16]{1,0:T(8,128)} %bitcast.13), custom_call_target="tpu_custom_call" | custom-call | tf_op jit(solution)/shard_map/pallas_call | solution.py:123
  1.2 1.9 %collective-permute-start = (bf16[32,2304]{1,0:T(8,128)(2,1)S(1)}, bf16[32,2304]{1,0:T(8,128)(2,1)S(1)}, u32[]{:S(2)}, u32[]{:S(2)}) collective-permute-start(bf16[32,2304]{1,0:T(8,128)(2,1)S(1)} %get-tuple-element.11), channel_id=1, source_target_pairs={{0,1},{1,0},{2,3},{3,2},{4,5},{5,4},{6,7},{7,6},{8,9},{9,8},{10,11... | collective-permute-start | bytes 442376 | tf_op jit(solution)/shard_map/ppermute | solution.py:136
  3.1 2.4 %collective-permute-start.1 = (bf16[896,2048]{1,0:T(8,128)(2,1)}, bf16[896,2048]{1,0:T(8,128)(2,1)S(1)}, u32[]{:S(2)}, u32[]{:S(2)}) collective-permute-start(bf16[896,2048]{1,0:T(8,128)(2,1)} %mine_ref), channel_id=1, source_target_pairs={{0,1},{1,0},{2,3},{3,2},{4,5},{5,4},{6,7},{7,6},{8,9},{9,8},{10,11... | collective-permute-start | bytes 11010056 | tf_op jit(solution)/shard_map/ppermute | solution.py:138
  5.5 0.0 collective-permute-done
  5.6 0.1 select_reduce_fusion.1
  5.7 0.1 fusion.3
  5.8 0.1 multiply_convert_fusion.1
  5.9 0.1 multiply_convert_fusion
  6.0 0.1 broadcast_in_dim.40
  6.1 0.1 pad_maximum_fusion
  6.2 68.1 %all-gather.1 = f16[512,4224]{1,0:T(8,128)(2,1)S(1)} all-gather(f16[32,4224]{1,0:T(8,128)(2,1)S(1)} %pad_maximum_fusion), channel_id=1, replica_groups=mesh['pair'=16,'y'=4,'x'=4,'core'=2] {'pair'}, dimensions={0}, use_global_device_ids=true | all-gather | bytes 4595712 | tf_op jit(solution)/shard_map/all_gather | solution.py:149
  74.3 0.0 copy-start
  74.3 0.0 copy-start.1
  74.3 0.6 convert_element_type.36.columns_ref
  74.9 0.0 collective-permute-done.1.theirs_ref
  74.9 0.1 copy-done
  75.0 1.4 %copy-done.1 = bf16[896,2048]{1,0:T(8,128)(2,1)S(1)} copy-done((bf16[896,2048]{1,0:T(8,128)(2,1)S(1)}, bf16[896,2048]{1,0:T(8,128)(2,1)}, u32[]{:S(2)}) %copy-start.1) | copy-done | bytes 3670040
  76.4 7.5 %shard_map.47 = s16[16,240,128]{2,1,0:T(8,128)(2,1)S(1)} custom-call(bf16[512,4224]{1,0:T(8,128)(2,1)S(1)} %convert_element_type.36.columns_ref, bf16[896,2048]{1,0:T(8,128)(2,1)S(1)} %copy-done.1, bf16[896,2048]{1,0:T(8,128)(2,1)S(1)} %collective-permute-done.1.theirs_ref, s32[7,16]{1,0:T(8,128)S(1)} %copy-done, s32[7,16]{1,0:T(8,128)S(1)} %slice_convert_fusion.keep_theirs_ref), custom_call_target="tpu_custom_call" | custom-call | flops 3758096384 | bytes 16777216 | tf_op jit(solution)/shard_map/pallas_call | solution.py:152
  83.9 18.6 %all_to_all.5 = s16[16,240,128]{2,1,0:T(8,128)(2,1)S(1)} all-to-all(s16[16,240,128]{2,1,0:T(8,128)(2,1)S(1)} %shard_map.47), channel_id=1, replica_groups=mesh['pair'=16,'y'=4,'x'=4,'core'=2] {'y','x'}, dimensions={0} | all-to-all | bytes 1966080 | tf_op jit(solution)/shard_map/all_to_all | solution.py:168
  102.5 0.3 convert_element_type.38
  102.8 0.1 fusion
  102.9 0.6 copy.8
  (2 shorter events, 0.0 us)
Async XLA Ops:
  1.2 4.3 %collective-permute-start = (bf16[32,2304]{1,0:T(8,128)(2,1)S(1)}, bf16[32,2304]{1,0:T(8,128)(2,1)S(1)}, u32[]{:S(2)}, u32[]{:S(2)}) collective-permute-start(bf16[32,2304]{1,0:T(8,128)(2,1)S(1)} %get-tuple-element.11), channel_id=1, source_target_pairs={{0,1},{1,0},{2,3},{3,2},{4,5},{5,4},{6,7},{7,6},{8,9},{9,8},{10,11... | collective-permute-start | bytes 442376 | tf_op jit(solution)/shard_map/ppermute | solution.py:136
  3.1 71.8 %collective-permute-start.1 = (bf16[896,2048]{1,0:T(8,128)(2,1)}, bf16[896,2048]{1,0:T(8,128)(2,1)S(1)}, u32[]{:S(2)}, u32[]{:S(2)}) collective-permute-start(bf16[896,2048]{1,0:T(8,128)(2,1)} %mine_ref), channel_id=1, source_target_pairs={{0,1},{1,0},{2,3},{3,2},{4,5},{5,4},{6,7},{7,6},{8,9},{9,8},{10,11... | collective-permute-start | bytes 11010056 | tf_op jit(solution)/shard_map/ppermute | solution.py:138
  74.3 0.7 copy-start
  74.3 2.1 %copy-start.1 = (bf16[896,2048]{1,0:T(8,128)(2,1)S(1)}, bf16[896,2048]{1,0:T(8,128)(2,1)}, u32[]{:S(2)}) copy-start(bf16[896,2048]{1,0:T(8,128)(2,1)} %mine_ref) | copy-start | bytes 11010052

commit v4 on v3

--- a/solution.py
+++ b/solution.py
@@ -64,34 +64,10 @@
     away_ref[:, depth + TILE_SIZE :] = tail_ref[...].astype(jnp.bfloat16)
 
 
-def masked_product(
-    columns_ref, mine_ref, theirs_ref, keep_mine_ref, keep_theirs_ref, out_ref, kept_ref, total_ref, code_ref, sems
-):
-    depth = mine_ref.shape[1]
-    loads = [
-        pltpu.make_async_copy(amps, kept_ref.at[part], sems.at[part]) for part, amps in enumerate((mine_ref, theirs_ref))
-    ]
-    for load in loads:
-        load.start()
-    scale = of_level(columns_ref[:, 2 * depth : 2 * depth + 1].astype(jnp.float32), -1)
-    for part, keep in enumerate((keep_mine_ref, keep_theirs_ref)):
-        loads[part].wait()
-        for row_tile in range(keep.shape[0]):
-            for tile in range(keep.shape[1]):
-                rows = slice(row_tile * TILE_SIZE, (row_tile + 1) * TILE_SIZE)
-                at = slice(tile * TILE_SIZE, (tile + 1) * TILE_SIZE)
-                kept_ref[part, rows, at] *= keep[row_tile, tile].astype(jnp.bfloat16)
-    total_ref[...] = scale * sum(
-        lax.dot_general(
-            columns_ref[:, part * depth : (part + 1) * depth],
-            kept_ref[part],
-            (((1,), (1,)), ((), ())),
-            preferred_element_type=jnp.float32,
-        )
-        for part in range(2)
-    )
-    pieces, row_tiles = out_ref.shape[0], keep_mine_ref.shape[0]
-    half = columns_ref.shape[0] // pieces
+def fixed_point(near_ref, far_ref, level_ref, out_ref, total_ref, code_ref):
+    total_ref[...] = of_level(level_ref[:, :1].astype(jnp.float32), -1) * (near_ref[...] + far_ref[...])
+    pieces, half = out_ref.shape[0], near_ref.shape[0] // out_ref.shape[0]
+    row_tiles = near_ref.shape[1] // TILE_SIZE
 
     def block(piece, tile):
         return total_ref[piece * half : (piece + 1) * half, tile * TILE_SIZE : (tile + 1) * TILE_SIZE]
@@ -119,7 +95,6 @@
     half = width // 2
 
     vmem, smem = pl.BlockSpec(memory_space=pltpu.VMEM), pl.BlockSpec(memory_space=pltpu.SMEM)
-    hbm = pl.BlockSpec(memory_space=pltpu.HBM)
     stay, away = pl.pallas_call(
         prepared,
         out_shape=(
@@ -137,7 +112,7 @@
     amplitudes, stay = lax.optimization_barrier((amplitudes, stay))
     amp_theirs = lax.ppermute(amplitudes, "core", OTHER_CORE)
     keep_at = depth + TILE_SIZE
-    keep_theirs = theirs[:row_tiles, keep_at : keep_at + depth_tiles].astype(jnp.int32)
+    keep_mine, keep_theirs = (part[:row_tiles, keep_at : keep_at + depth_tiles] for part in (away, theirs))
 
     levels = [part[:, depth : depth + 1].astype(jnp.float32) for part in (stay, theirs)]
     level = jnp.minimum(*levels)
@@ -148,23 +123,26 @@
     ).astype(jnp.float16)
     columns = lax.all_gather(sent, "pair", axis=0, tiled=True).astype(jnp.bfloat16)
 
+    def product(columns, amps, keep):
+        keep = lax.optimization_barrier(jnp.repeat(keep, TILE_SIZE, axis=1))
+        amp_kept = (amps.reshape(row_tiles, TILE_SIZE, depth) * keep[:, None, :]).reshape(amps.shape)
+        return lax.dot_general(columns, amp_kept, (((1,), (1,)), ((), ())), preferred_element_type=jnp.float32)
+
+    far = product(columns[:, depth : 2 * depth], amp_theirs, keep_theirs)
+    columns, far, keep_mine = lax.optimization_barrier((columns, far, keep_mine))
+    near = product(columns[:, :depth], amplitudes, keep_mine)
     pieces = columns.shape[0] // half
     partial_value = pl.pallas_call(
-        masked_product,
+        fixed_point,
         out_shape=jax.ShapeDtypeStruct((pieces, row_tiles * half + CODE_ROWS, TILE_SIZE), jnp.int16),
-        in_specs=[vmem, hbm, hbm, smem, smem],
+        in_specs=[vmem, vmem, vmem],
         out_specs=vmem,
         scratch_shapes=[
-            pltpu.VMEM((2, rows, depth), jnp.bfloat16),
             pltpu.VMEM((columns.shape[0], rows), jnp.float32),
             pltpu.VMEM((pieces * CODE_ROWS, TILE_SIZE), jnp.float32),
-            pltpu.SemaphoreType.DMA((2,)),
         ],
-        compiler_params=pltpu.CompilerParams(vmem_limit_bytes=32 * 1024 * 1024),
-        cost_estimate=pl.CostEstimate(
-            flops=4 * columns.shape[0] * rows * depth, bytes_accessed=16 * 1024 * 1024, transcendentals=0
-        ),
-    )(columns, amplitudes, amp_theirs, mask_amp, keep_theirs)
+        compiler_params=pltpu.CompilerParams(vmem_limit_bytes=16 * 1024 * 1024),
+    )(near, far, columns[:, 2 * depth :])
     partial_value = lax.all_to_all(partial_value, PLANE, 0, 0, tiled=True).astype(jnp.float32)
     steps = jnp.exp2(partial_value[:, row_tiles * half : row_tiles * half + row_tiles] * (1.0 / OCTAVE))
     fixed = partial_value[:, : row_tiles * half].reshape(pieces, row_tiles, half, TILE_SIZE)

time: 104 us -> 101 us (0.971)
  Pallas kernels: 8.74 us -> 1.88 us
  matrix products: 0 us -> 4.72 us
  local copies, waits for them, and re-layouts: 2.18 us -> 0.91 us
    pallas_call x1, Pallas kernels: 7.55 us -> 0.69 us  [shards(): pl.pallas_call(fixed_point, out_shape=jax.ShapeDtypeStruct((pieces, row_t...]
    dot_general x0 -> x2, matrix products: none -> 4.72 us  [product(): lax.dot_general(columns, amp_kept, (((1,), (1,)), ((), ())), preferred_el...]
    unnamed x4 -> x6, local copies, waits for them, and re-layouts: 1.47 us -> 0.18 us
where the time goes in v4:
time: 101 us
  blocking collectives  86.7 us (86%)
  matrix products  4.72 us (5%)
  starting transfers between devices  4.33 us (4%)
  other arithmetic  2 us (2%)
  Pallas kernels  1.88 us (2%)
    all_gather x1, blocking collectives, shards(): lax.all_gather(sent, 'pair', axis=0, tiled=True).astype(jnp.bfloat16)  68.1 us
    all_to_all x1, blocking collectives, shards(): lax.all_to_all(partial_value, PLANE, 0, 0, tiled=True).astype(jnp.float32)  18.6 us
    dot_general x2, matrix products, product(): lax.dot_general(columns, amp_kept, (((1,), (1,)), ((), ())), preferred_el...  4.72 us
    ppermute x1, starting transfers between devices, shards(): amp_theirs = lax.ppermute(amplitudes, 'core', OTHER_CORE)  2.41 us
  transfers between devices with their start and end apart: 2, of which 0 were waited for; matrix products, arithmetic and copies ran while one was open for 1% of the time, Pallas kernels for 0%

profile of v4, /device:TPU:2, one launch (start us, length us, event | category | flops | bytes accessed | tf_op | source)
XLA Modules:
  0.0 100.7 jit_solution(5664083198994152981)
XLA Ops:
  0.0 1.2 %shard_map.46 = (bf16[32,2176]{1,0:T(8,128)(2,1)S(1)}, bf16[32,2304]{1,0:T(8,128)(2,1)S(1)}) custom-call(bf16[64,2048]{1,0:T(8,128)(2,1)} %bitcast.27, s32[7,16]{1,0:T(8,128)} %keep_amp_ref.1, s32[8,16]{1,0:T(8,128)} %bitcast.31), custom_call_target="tpu_custom_call" | custom-call | tf_op jit(solution)/shard_map/pallas_call | solution.py:98
  1.2 1.9 %collective-permute-start = (bf16[32,2304]{1,0:T(8,128)(2,1)S(1)}, bf16[32,2304]{1,0:T(8,128)(2,1)S(1)}, u32[]{:S(2)}, u32[]{:S(2)}) collective-permute-start(bf16[32,2304]{1,0:T(8,128)(2,1)S(1)} %get-tuple-element.14), channel_id=1, source_target_pairs={{0,1},{1,0},{2,3},{3,2},{4,5},{5,4},{6,7},{7,6},{8,9},{9,8},{10,11... | collective-permute-start | bytes 442376 | tf_op jit(solution)/shard_map/ppermute | solution.py:111
  3.1 2.4 %collective-permute-start.1 = (bf16[896,2048]{1,0:T(8,128)(2,1)}, bf16[896,2048]{1,0:T(8,128)(2,1)S(1)}, u32[]{:S(2)}, u32[]{:S(2)}) collective-permute-start(bf16[896,2048]{1,0:T(8,128)(2,1)} %param.4), channel_id=1, source_target_pairs={{0,1},{1,0},{2,3},{3,2},{4,5},{5,4},{6,7},{7,6},{8,9},{9,8},{10,11... | collective-permute-start | bytes 11010056 | tf_op jit(solution)/shard_map/ppermute | solution.py:113
  5.6 0.0 collective-permute-done
  5.6 0.1 select_reduce_fusion.1
  5.7 0.1 fusion.7
  5.8 0.1 multiply_convert_fusion.1
  5.9 0.1 multiply_convert_fusion
  6.0 0.1 broadcast_in_dim.48
  6.1 0.1 pad_maximum_fusion
  6.2 68.1 %all-gather.1 = f16[512,4224]{1,0:T(8,128)(2,1)S(1)} all-gather(f16[32,4224]{1,0:T(8,128)(2,1)S(1)} %pad_maximum_fusion), channel_id=1, replica_groups=mesh['pair'=16,'y'=4,'x'=4,'core'=2] {'pair'}, dimensions={0}, use_global_device_ids=true | all-gather | bytes 4595712 | tf_op jit(solution)/shard_map/all_gather | solution.py:124
  74.3 0.5 convert_element_type.33
  74.9 0.1 broadcast_bitcast_fusion.1
  75.0 0.3 bitcast_multiply_fusion.1
  75.3 0.0 copy-start
  75.3 2.4 %fusion.far_ref = f32[512,896]{1,0:T(8,128)S(1)} fusion(bf16[896,2048]{1,0:T(8,128)(2,1)S(1)} %bitcast_multiply_fusion.1, bf16[512,4224]{1,0:T(8,128)(2,1)S(1)} %convert_element_type.33), kind=kOutput, calls=%fused_computation.2 | convolution fusion | flops 1879048192 | bytes 7602176 | tf_op jit(solution)/shard_map/dot_general | solution.py:129
  77.6 0.1 broadcast_bitcast_fusion
  77.8 0.3 bitcast_multiply_fusion
  78.0 2.4 %fusion.2.near_ref = f32[512,896]{1,0:T(8,128)S(1)} fusion(bf16[896,2048]{1,0:T(8,128)(2,1)S(1)} %bitcast_multiply_fusion, bf16[512,4224]{1,0:T(8,128)(2,1)S(1)} %convert_element_type.33), kind=kOutput, calls=%fused_computation.4 | convolution fusion | flops 1879048192 | bytes 7602176 | tf_op jit(solution)/shard_map/dot_general | solution.py:129
  80.4 0.7 shard_map.47
  81.1 18.6 %all_to_all.5 = s16[16,240,128]{2,1,0:T(8,128)(2,1)S(1)} all-to-all(s16[16,240,128]{2,1,0:T(8,128)(2,1)S(1)} %shard_map.47), channel_id=1, replica_groups=mesh['pair'=16,'y'=4,'x'=4,'core'=2] {'y','x'}, dimensions={0} | all-to-all | bytes 1966080 | tf_op jit(solution)/shard_map/all_to_all | solution.py:146
  99.7 0.3 convert_element_type.34
  99.9 0.1 fusion.4
  100.1 0.6 copy.12
  (8 shorter events, 0.1 us)
Async XLA Ops:
  1.2 4.4 %collective-permute-start = (bf16[32,2304]{1,0:T(8,128)(2,1)S(1)}, bf16[32,2304]{1,0:T(8,128)(2,1)S(1)}, u32[]{:S(2)}, u32[]{:S(2)}) collective-permute-start(bf16[32,2304]{1,0:T(8,128)(2,1)S(1)} %get-tuple-element.14), channel_id=1, source_target_pairs={{0,1},{1,0},{2,3},{3,2},{4,5},{5,4},{6,7},{7,6},{8,9},{9,8},{10,11... | collective-permute-start | bytes 442376 | tf_op jit(solution)/shard_map/ppermute | solution.py:111
  3.1 71.9 %collective-permute-start.1 = (bf16[896,2048]{1,0:T(8,128)(2,1)}, bf16[896,2048]{1,0:T(8,128)(2,1)S(1)}, u32[]{:S(2)}, u32[]{:S(2)}) collective-permute-start(bf16[896,2048]{1,0:T(8,128)(2,1)} %param.4), channel_id=1, source_target_pairs={{0,1},{1,0},{2,3},{3,2},{4,5},{5,4},{6,7},{7,6},{8,9},{9,8},{10,11... | collective-permute-start | bytes 11010056 | tf_op jit(solution)/shard_map/ppermute | solution.py:113
  75.3 2.5 %copy-start = (bf16[896,2048]{1,0:T(8,128)(2,1)S(1)}, bf16[896,2048]{1,0:T(8,128)(2,1)}, u32[]{:S(2)}) copy-start(bf16[896,2048]{1,0:T(8,128)(2,1)} %param.4) | copy-start | bytes 11010052

commit v5 on v4

--- a/solution.py
+++ b/solution.py
@@ -12,10 +12,6 @@
 LIFT = 2.0**16
 FIRST_SCALE = 2.0**18
 FIRST_LIMIT = 2.0**-19
-STEPS = 32000.0
-OCTAVE = 8.0
-CODE_ROWS = 16
-SMALLEST = 1e-33
 
 
 def column_levels(largest):
@@ -64,30 +60,6 @@
     away_ref[:, depth + TILE_SIZE :] = tail_ref[...].astype(jnp.bfloat16)
 
 
-def fixed_point(near_ref, far_ref, level_ref, out_ref, total_ref, code_ref):
-    total_ref[...] = of_level(level_ref[:, :1].astype(jnp.float32), -1) * (near_ref[...] + far_ref[...])
-    pieces, half = out_ref.shape[0], near_ref.shape[0] // out_ref.shape[0]
-    row_tiles = near_ref.shape[1] // TILE_SIZE
-
-    def block(piece, tile):
-        return total_ref[piece * half : (piece + 1) * half, tile * TILE_SIZE : (tile + 1) * TILE_SIZE]
-
-    code_ref[...] = jnp.zeros_like(code_ref)
-    for piece in range(pieces):
-        for tile in range(row_tiles):
-            largest = jnp.max(jnp.abs(block(piece, tile)), axis=0, keepdims=True)
-            code_ref[piece * CODE_ROWS + tile : piece * CODE_ROWS + tile + 1, :] = largest
-    codes = jnp.ceil(jnp.log2(jnp.maximum(code_ref[...], SMALLEST) / STEPS) * OCTAVE)
-    code_ref[...] = jnp.exp2(codes * (-1.0 / OCTAVE))
-    codes = codes.astype(jnp.int32).astype(jnp.int16)
-    for piece in range(pieces):
-        for tile in range(row_tiles):
-            inverse = code_ref[piece * CODE_ROWS + tile : piece * CODE_ROWS + tile + 1, :]
-            fixed = jnp.round(block(piece, tile) * inverse).astype(jnp.int32).astype(jnp.int16)
-            out_ref[piece, tile * half : (tile + 1) * half, :] = fixed
-        out_ref[piece, row_tiles * half :, :] = codes[piece * CODE_ROWS : (piece + 1) * CODE_ROWS]
-
-
 def shards(amplitudes, mask_amp, integrals, mask_int):
     row_tiles, depth_tiles = mask_amp.shape
     rows = amplitudes.shape[0]
@@ -131,23 +103,10 @@
     far = product(columns[:, depth : 2 * depth], amp_theirs, keep_theirs)
     columns, far, keep_mine = lax.optimization_barrier((columns, far, keep_mine))
     near = product(columns[:, :depth], amplitudes, keep_mine)
-    pieces = columns.shape[0] // half
-    partial_value = pl.pallas_call(
-        fixed_point,
-        out_shape=jax.ShapeDtypeStruct((pieces, row_tiles * half + CODE_ROWS, TILE_SIZE), jnp.int16),
-        in_specs=[vmem, vmem, vmem],
-        out_specs=vmem,
-        scratch_shapes=[
-            pltpu.VMEM((columns.shape[0], rows), jnp.float32),
-            pltpu.VMEM((pieces * CODE_ROWS, TILE_SIZE), jnp.float32),
-        ],
-        compiler_params=pltpu.CompilerParams(vmem_limit_bytes=16 * 1024 * 1024),
-    )(near, far, columns[:, 2 * depth :])
-    partial_value = lax.all_to_all(partial_value, PLANE, 0, 0, tiled=True).astype(jnp.float32)
-    steps = jnp.exp2(partial_value[:, row_tiles * half : row_tiles * half + row_tiles] * (1.0 / OCTAVE))
-    fixed = partial_value[:, : row_tiles * half].reshape(pieces, row_tiles, half, TILE_SIZE)
-    total = jnp.sum(fixed * steps[:, :, None, :], axis=0)
-    return total.astype(jnp.bfloat16).transpose(0, 2, 1).reshape(rows, half)
+    scale = of_level(columns[:, 2 * depth : 2 * depth + 1].astype(jnp.float32), -1)
+    near, far = lax.optimization_barrier((near, far))
+    pieces = lax.all_to_all(scale * (near + far), PLANE, 0, 0, tiled=True)
+    return jnp.sum(pieces.reshape(-1, half, rows), axis=0).astype(jnp.bfloat16).T
 
 
 def solution(mesh):

time: 101 us -> 108 us (1.069)
  the two profiles are of different devices: /device:TPU:2 before, /device:TPU:32 now
where the time goes in v5:
time: 108 us
  blocking collectives  94.5 us (88%)
  matrix products  4.72 us (4%)
  starting transfers between devices  4.33 us (4%)
  other arithmetic  2.83 us (3%)
  Pallas kernels  1.19 us (1%)
    all_gather x1, blocking collectives, shards(): lax.all_gather(sent, 'pair', axis=0, tiled=True).astype(jnp.bfloat16)  66.6 us
    all_to_all x1, blocking collectives, shards(): pieces = lax.all_to_all(scale * (near + far), PLANE, 0, 0, tiled=True)  27.9 us
    dot_general x2, matrix products, product(): lax.dot_general(columns, amp_kept, (((1,), (1,)), ((), ())), preferred_el...  4.72 us
    ppermute x1, starting transfers between devices, shards(): amp_theirs = lax.ppermute(amplitudes, 'core', OTHER_CORE)  2.41 us
  transfers between devices with their start and end apart: 2, of which 0 were waited for; matrix products, arithmetic and copies ran while one was open for 1% of the time, Pallas kernels for 0%

profile of v5, /device:TPU:32, one launch (start us, length us, event | category | flops | bytes accessed | tf_op | source)
XLA Modules:
  0.0 108.0 jit_solution(1463435866016559589)
XLA Ops:
  0.0 1.2 %shard_map.46 = (bf16[32,2176]{1,0:T(8,128)(2,1)S(1)}, bf16[32,2304]{1,0:T(8,128)(2,1)S(1)}) custom-call(bf16[64,2048]{1,0:T(8,128)(2,1)} %bitcast.23, s32[7,16]{1,0:T(8,128)} %keep_amp_ref.1, s32[8,16]{1,0:T(8,128)} %bitcast.26), custom_call_target="tpu_custom_call" | custom-call | tf_op jit(solution)/shard_map/pallas_call | solution.py:70
  1.2 1.9 %collective-permute-start = (bf16[32,2304]{1,0:T(8,128)(2,1)S(1)}, bf16[32,2304]{1,0:T(8,128)(2,1)S(1)}, u32[]{:S(2)}, u32[]{:S(2)}) collective-permute-start(bf16[32,2304]{1,0:T(8,128)(2,1)S(1)} %get-tuple-element.16), channel_id=1, source_target_pairs={{0,1},{1,0},{2,3},{3,2},{4,5},{5,4},{6,7},{7,6},{8,9},{9,8},{10,11... | collective-permute-start | bytes 442376 | tf_op jit(solution)/shard_map/ppermute | solution.py:83
  3.1 2.4 %collective-permute-start.1 = (bf16[896,2048]{1,0:T(8,128)(2,1)}, bf16[896,2048]{1,0:T(8,128)(2,1)S(1)}, u32[]{:S(2)}, u32[]{:S(2)}) collective-permute-start(bf16[896,2048]{1,0:T(8,128)(2,1)} %param.4), channel_id=1, source_target_pairs={{0,1},{1,0},{2,3},{3,2},{4,5},{5,4},{6,7},{7,6},{8,9},{9,8},{10,11... | collective-permute-start | bytes 11010056 | tf_op jit(solution)/shard_map/ppermute | solution.py:85
  5.6 0.0 collective-permute-done
  5.6 0.1 select_reduce_fusion.2
  5.7 0.1 fusion.5
  5.8 0.1 multiply_convert_fusion.1
  5.9 0.1 multiply_convert_fusion
  6.0 0.1 broadcast_in_dim.69
  6.1 0.1 pad_maximum_fusion
  6.2 66.6 %all-gather.1 = f16[512,4224]{1,0:T(8,128)(2,1)S(1)} all-gather(f16[32,4224]{1,0:T(8,128)(2,1)S(1)} %pad_maximum_fusion), channel_id=1, replica_groups=mesh['pair'=16,'y'=4,'x'=4,'core'=2] {'pair'}, dimensions={0}, use_global_device_ids=true | all-gather | bytes 4595712 | tf_op jit(solution)/shard_map/all_gather | solution.py:96
  72.8 0.5 convert_element_type.30
  73.4 0.1 broadcast_bitcast_fusion.1
  73.5 0.0 collective-permute-done.1
  73.5 0.3 bitcast_multiply_fusion.1
  73.7 0.0 copy-start
  73.7 2.4 %fusion = f32[512,896]{1,0:T(8,128)S(1)} fusion(bf16[896,2048]{1,0:T(8,128)(2,1)S(1)} %bitcast_multiply_fusion.1, bf16[512,4224]{1,0:T(8,128)(2,1)S(1)} %convert_element_type.30), kind=kOutput, calls=%fused_computation.2 | convolution fusion | flops 1879048192 | bytes 7602176 | tf_op jit(solution)/shard_map/dot_general | solution.py:101
  76.1 0.1 broadcast_bitcast_fusion
  76.2 0.3 bitcast_multiply_fusion
  76.5 0.2 select_reduce_fusion
  76.7 2.4 %fusion.2 = f32[512,896]{1,0:T(8,128)S(1)} fusion(bf16[896,2048]{1,0:T(8,128)(2,1)S(1)} %bitcast_multiply_fusion, bf16[512,4224]{1,0:T(8,128)(2,1)S(1)} %convert_element_type.30), kind=kOutput, calls=%fused_computation.4 | convolution fusion | flops 1879048192 | bytes 7602176 | tf_op jit(solution)/shard_map/dot_general | solution.py:101
  79.1 0.3 add_multiply_fusion
  79.4 27.9 %all_to_all.9 = f32[16,32,896]{2,1,0:T(8,128)S(1)} all-to-all(f32[16,32,896]{2,1,0:T(8,128)S(1)} %bitcast.22), channel_id=1, replica_groups=mesh['pair'=16,'y'=4,'x'=4,'core'=2] {'y','x'}, dimensions={0} | all-to-all | bytes 3670016 | tf_op jit(solution)/shard_map/all_to_all | solution.py:108
  107.3 0.7 reduce_sum.9
  (5 shorter events, 0.0 us)
Async XLA Ops:
  1.2 4.4 %collective-permute-start = (bf16[32,2304]{1,0:T(8,128)(2,1)S(1)}, bf16[32,2304]{1,0:T(8,128)(2,1)S(1)}, u32[]{:S(2)}, u32[]{:S(2)}) collective-permute-start(bf16[32,2304]{1,0:T(8,128)(2,1)S(1)} %get-tuple-element.16), channel_id=1, source_target_pairs={{0,1},{1,0},{2,3},{3,2},{4,5},{5,4},{6,7},{7,6},{8,9},{9,8},{10,11... | collective-permute-start | bytes 442376 | tf_op jit(solution)/shard_map/ppermute | solution.py:83
  3.1 70.3 %collective-permute-start.1 = (bf16[896,2048]{1,0:T(8,128)(2,1)}, bf16[896,2048]{1,0:T(8,128)(2,1)S(1)}, u32[]{:S(2)}, u32[]{:S(2)}) collective-permute-start(bf16[896,2048]{1,0:T(8,128)(2,1)} %param.4), channel_id=1, source_target_pairs={{0,1},{1,0},{2,3},{3,2},{4,5},{5,4},{6,7},{7,6},{8,9},{9,8},{10,11... | collective-permute-start | bytes 11010056 | tf_op jit(solution)/shard_map/ppermute | solution.py:85
  73.7 2.5 %copy-start = (bf16[896,2048]{1,0:T(8,128)(2,1)S(1)}, bf16[896,2048]{1,0:T(8,128)(2,1)}, u32[]{:S(2)}) copy-start(bf16[896,2048]{1,0:T(8,128)(2,1)} %param.4) | copy-start | bytes 11010052

commit v6 on v4

--- a/solution.py
+++ b/solution.py
@@ -12,6 +12,7 @@
 LIFT = 2.0**16
 FIRST_SCALE = 2.0**18
 FIRST_LIMIT = 2.0**-19
+TAIL = 64
 STEPS = 32000.0
 OCTAVE = 8.0
 CODE_ROWS = 16
@@ -29,13 +30,6 @@
     value = jnp.full_like(level, FIRST_SCALE**sign)
     for step in range(1, LEVELS):
         value = jnp.where(level == step, (FIRST_SCALE * LIFT**step) ** sign, value)
-    return value
-
-
-def lowered(steps):
-    value = jnp.ones_like(steps)
-    for step in range(1, LEVELS):
-        value = jnp.where(steps == step, LIFT**-step, value)
     return value
 
 
@@ -65,7 +59,10 @@
 
 
 def fixed_point(near_ref, far_ref, level_ref, out_ref, total_ref, code_ref):
-    total_ref[...] = of_level(level_ref[:, :1].astype(jnp.float32), -1) * (near_ref[...] + far_ref[...])
+    near_scale, far_scale = (
+        of_level(level_ref[:, lane : lane + 1].astype(jnp.float32), -1) for lane in (0, TAIL)
+    )
+    total_ref[...] = near_scale * near_ref[...] + far_scale * far_ref[...]
     pieces, half = out_ref.shape[0], near_ref.shape[0] // out_ref.shape[0]
     row_tiles = near_ref.shape[1] // TILE_SIZE
 
@@ -114,13 +111,11 @@
     keep_at = depth + TILE_SIZE
     keep_mine, keep_theirs = (part[:row_tiles, keep_at : keep_at + depth_tiles] for part in (away, theirs))
 
-    levels = [part[:, depth : depth + 1].astype(jnp.float32) for part in (stay, theirs)]
-    level = jnp.minimum(*levels)
-    sent = jnp.concatenate(
-        [part[:, :depth].astype(jnp.float32) * lowered(own - level) for part, own in zip((stay, theirs), levels)]
-        + [jnp.broadcast_to(level, (half, TILE_SIZE))],
-        axis=1,
-    ).astype(jnp.float16)
+    stay, theirs = (part[:, : depth + TAIL].astype(jnp.float32) for part in (stay, theirs))
+    theirs = lax.optimization_barrier(theirs)
+    levels = lax.optimization_barrier(jnp.concatenate([part[:, depth:] for part in (stay, theirs)], axis=1))
+    blocks = lax.optimization_barrier([part[:, :depth].astype(jnp.float16) for part in (stay, theirs)])
+    sent = jnp.concatenate([*blocks, levels.astype(jnp.float16)], axis=1)
     columns = lax.all_gather(sent, "pair", axis=0, tiled=True).astype(jnp.bfloat16)
 
     def product(columns, amps, keep):

time: 101 us -> 101 us (level)
  no operation moved by 1% of the time
where the time goes in v6:
time: 101 us; the launch traced here: 100 us
  blocking collectives  86.7 us (86%)
  matrix products  4.72 us (5%)
  starting transfers between devices  4.33 us (4%)
  Pallas kernels  1.98 us (2%)
  other arithmetic  1.72 us (2%)
    all_gather x1, blocking collectives, shards(): lax.all_gather(sent, 'pair', axis=0, tiled=True).astype(jnp.bfloat16)  68.1 us
    all_to_all x1, blocking collectives, shards(): lax.all_to_all(partial_value, PLANE, 0, 0, tiled=True).astype(jnp.float32)  18.6 us
    dot_general x2, matrix products, product(): lax.dot_general(columns, amp_kept, (((1,), (1,)), ((), ())), preferred_el...  4.72 us
    ppermute x1, starting transfers between devices, shards(): amp_theirs = lax.ppermute(amplitudes, 'core', OTHER_CORE)  2.41 us
  transfers between devices with their start and end apart: 2, of which 0 were waited for; matrix products, arithmetic and copies ran while one was open for 1% of the time, Pallas kernels for 0%

profile of v6, /device:TPU:2, one launch (start us, length us, event | category | flops | bytes accessed | tf_op | source)
XLA Modules:
  0.0 100.5 jit_solution(14955760113637787336)
XLA Ops:
  0.0 1.2 %shard_map.46 = (bf16[32,2176]{1,0:T(8,128)(2,1)S(1)}, bf16[32,2304]{1,0:T(8,128)(2,1)S(1)}) custom-call(bf16[64,2048]{1,0:T(8,128)(2,1)} %bitcast.27, s32[7,16]{1,0:T(8,128)} %keep_amp_ref.1, s32[8,16]{1,0:T(8,128)} %bitcast.31), custom_call_target="tpu_custom_call" | custom-call | tf_op jit(solution)/shard_map/pallas_call | solution.py:95
  1.2 1.9 %collective-permute-start = (bf16[32,2304]{1,0:T(8,128)(2,1)S(1)}, bf16[32,2304]{1,0:T(8,128)(2,1)S(1)}, u32[]{:S(2)}, u32[]{:S(2)}) collective-permute-start(bf16[32,2304]{1,0:T(8,128)(2,1)S(1)} %get-tuple-element.16), channel_id=1, source_target_pairs={{0,1},{1,0},{2,3},{3,2},{4,5},{5,4},{6,7},{7,6},{8,9},{9,8},{10,11... | collective-permute-start | bytes 442376 | tf_op jit(solution)/shard_map/ppermute | solution.py:108
  3.1 2.4 %collective-permute-start.1 = (bf16[896,2048]{1,0:T(8,128)(2,1)}, bf16[896,2048]{1,0:T(8,128)(2,1)S(1)}, u32[]{:S(2)}, u32[]{:S(2)}) collective-permute-start(bf16[896,2048]{1,0:T(8,128)(2,1)} %param.4), channel_id=1, source_target_pairs={{0,1},{1,0},{2,3},{3,2},{4,5},{5,4},{6,7},{7,6},{8,9},{9,8},{10,11... | collective-permute-start | bytes 11010056 | tf_op jit(solution)/shard_map/ppermute | solution.py:110
  5.6 0.0 collective-permute-done
  5.7 0.1 pad_maximum_fusion.1
  5.8 0.1 pad_maximum_fusion
  5.9 68.1 %all-gather.1 = f16[512,4224]{1,0:T(8,128)(2,1)S(1)} all-gather(f16[32,4224]{1,0:T(8,128)(2,1)S(1)} %pad_maximum_fusion), channel_id=1, replica_groups=mesh['pair'=16,'y'=4,'x'=4,'core'=2] {'pair'}, dimensions={0}, use_global_device_ids=true | all-gather | bytes 4595712 | tf_op jit(solution)/shard_map/all_gather | solution.py:119
  74.0 0.5 convert_element_type.30
  74.6 0.1 broadcast_bitcast_fusion.1
  74.7 0.0 collective-permute-done.1
  74.7 0.3 bitcast_multiply_fusion.1
  74.9 0.0 copy-start
  75.0 2.4 %fusion.far_ref = f32[512,896]{1,0:T(8,128)S(1)} fusion(bf16[896,2048]{1,0:T(8,128)(2,1)S(1)} %bitcast_multiply_fusion.1, bf16[512,4224]{1,0:T(8,128)(2,1)S(1)} %convert_element_type.30), kind=kOutput, calls=%fused_computation.2 | convolution fusion | flops 1879048192 | bytes 7602176 | tf_op jit(solution)/shard_map/dot_general | solution.py:124
  77.3 0.1 broadcast_bitcast_fusion
  77.4 0.0 copy-done
  77.4 0.3 bitcast_multiply_fusion
  77.7 2.4 %fusion.2.near_ref = f32[512,896]{1,0:T(8,128)S(1)} fusion(bf16[896,2048]{1,0:T(8,128)(2,1)S(1)} %bitcast_multiply_fusion, bf16[512,4224]{1,0:T(8,128)(2,1)S(1)} %convert_element_type.30), kind=kOutput, calls=%fused_computation.4 | convolution fusion | flops 1879048192 | bytes 7602176 | tf_op jit(solution)/shard_map/dot_general | solution.py:124
  80.1 0.8 shard_map.47
  80.9 18.6 %all_to_all.5 = s16[16,240,128]{2,1,0:T(8,128)(2,1)S(1)} all-to-all(s16[16,240,128]{2,1,0:T(8,128)(2,1)S(1)} %shard_map.47), channel_id=1, replica_groups=mesh['pair'=16,'y'=4,'x'=4,'core'=2] {'y','x'}, dimensions={0} | all-to-all | bytes 1966080 | tf_op jit(solution)/shard_map/all_to_all | solution.py:141
  99.4 0.3 convert_element_type.31
  99.7 0.1 fusion.4
  99.9 0.6 copy.12
  (12 shorter events, 0.1 us)
Async XLA Ops:
  1.2 4.4 %collective-permute-start = (bf16[32,2304]{1,0:T(8,128)(2,1)S(1)}, bf16[32,2304]{1,0:T(8,128)(2,1)S(1)}, u32[]{:S(2)}, u32[]{:S(2)}) collective-permute-start(bf16[32,2304]{1,0:T(8,128)(2,1)S(1)} %get-tuple-element.16), channel_id=1, source_target_pairs={{0,1},{1,0},{2,3},{3,2},{4,5},{5,4},{6,7},{7,6},{8,9},{9,8},{10,11... | collective-permute-start | bytes 442376 | tf_op jit(solution)/shard_map/ppermute | solution.py:108
  3.1 71.5 %collective-permute-start.1 = (bf16[896,2048]{1,0:T(8,128)(2,1)}, bf16[896,2048]{1,0:T(8,128)(2,1)S(1)}, u32[]{:S(2)}, u32[]{:S(2)}) collective-permute-start(bf16[896,2048]{1,0:T(8,128)(2,1)} %param.4), channel_id=1, source_target_pairs={{0,1},{1,0},{2,3},{3,2},{4,5},{5,4},{6,7},{7,6},{8,9},{9,8},{10,11... | collective-permute-start | bytes 11010056 | tf_op jit(solution)/shard_map/ppermute | solution.py:110
  74.9 2.5 %copy-start = (bf16[896,2048]{1,0:T(8,128)(2,1)S(1)}, bf16[896,2048]{1,0:T(8,128)(2,1)}, u32[]{:S(2)}) copy-start(bf16[896,2048]{1,0:T(8,128)(2,1)} %param.4) | copy-start | bytes 11010052
